TPU v7x, 32 devices: a whole 2x2x4 slice. The times are simulated.
32 devices in a mesh: group: 2 (over y), replica: 16 (over z, x, core), tensor: 1.
Axes of the slice: x: 2, y: 2, z: 4, core: 2. Of those that a mesh axis runs over, the one named last changes fastest.
Arguments:
- tokens: bfloat16 [32768, 8192], P(('group', 'replica'), 'tensor'), parts along dimension 0, may hold values from -6 to 6
- token_adapter: int32 [32768, 1], P(('group', 'replica')), parts along dimension 0, may hold values from 0 to 31; in each aligned block of 1024 rows (0 to 1023, 1024 to 2047, ...) at most 64 rows name the same one
- adapter_position: int32 [64], P('group'), parts along dimension 0, may hold values from 0 to 31, each once
- replica_live_rows: int32 [32], P(('group', 'replica')), parts along dimension 0, may hold values from 512 to 1024, as said below
- value_weight: bfloat16 [8192, 1024], P('tensor'), may hold values from -0.0625 to 0.0625
- adapter_down_weight: bfloat16 [64, 64, 8192], P(('group', 'replica'), None, 'tensor'), parts along dimension 0, may hold values from -0.0625 to 0.0625
- adapter_up_weight: bfloat16 [64, 64, 1024], P(('group', 'replica'), None, 'tensor'), parts along dimension 0, may hold values from -0.75 to 0.75
Outputs:
- values: bfloat16 [32768, 1024], P(('group', 'replica'), 'tensor'), parts along dimension 0
There are 2 independent parts, one for each index of `group`. A program takes and returns all parts, laid end to end along the dimension named above; an argument that names none is the same for every part. Nothing has to cross between parts.
Inputs may be any that keep to these rules, and one draw needn't show every extreme that they name: `token_adapter`: within each replica's 1024 rows no adapter is named by more than 64 rows, a bound that some block reaches. `replica_live_rows`: some replica has all 1024 rows live.
All inputs are finite; a program needn't handle non-finite values.
Results may differ from a plain program's by a relative error of at most 0.0045.
Values may be sent and summed in bfloat16 or wider, within the bound.
A program may use at most 192 MiB of HBM per device.

v0:
```python
import jax
import jax.numpy as jnp
from jax import lax
from jax.sharding import PartitionSpec as P


def shards(
    tokens,
    token_adapter,
    adapter_position,
    replica_live_rows,
    value_weight,
    adapter_down_weight,
    adapter_up_weight,
):
    row_count = tokens.shape[0]
    feat_cols = tokens.shape[1]
    output_columns = adapter_up_weight.shape[2]
    adapter_count = adapter_position.shape[0]
    capacity = 2 * row_count // adapter_count
    id_match = token_adapter == jnp.arange(adapter_count, dtype=jnp.int32)[None, :]
    slot_of = jnp.sum(jnp.where(id_match, adapter_position[None, :], 0), axis=1)
    slot_hot = (slot_of[:, None] == jnp.arange(adapter_count, dtype=jnp.int32)[None, :]).astype(
        jnp.int32
    )
    before = jnp.cumsum(slot_hot, axis=0) - slot_hot
    position = jnp.sum(before * slot_hot, axis=1)
    destination_rows = slot_of * capacity + position
    alive_mask = jnp.arange(row_count, dtype=jnp.int32) < replica_live_rows[0]
    base_terms = jnp.dot(tokens, value_weight, preferred_element_type=jnp.float32)
    base_output = lax.psum_scatter(base_terms, "tensor", scatter_dimension=1, tiled=True)
    sending = jnp.where(alive_mask[:, None], tokens, jnp.zeros_like(tokens))
    buffer = (
        jnp.zeros((adapter_count * capacity, feat_cols), jnp.bfloat16)
        .at[destination_rows]
        .set(sending, mode="drop")
    )
    every_down, every_up = (
        lax.all_gather(adapter_down_weight, "replica", axis=0, tiled=True),
        lax.all_gather(adapter_up_weight, "replica", axis=0, tiled=True),
    )
    own_rows = buffer.reshape(adapter_count, capacity, feat_cols)
    partial_value = jnp.einsum(
        "acd,ard->acr", own_rows, every_down, preferred_element_type=jnp.float32
    )
    reduced_rows = lax.psum(partial_value, "tensor").astype(jnp.bfloat16)
    widened_output = jnp.einsum(
        "acr,are->ace", reduced_rows, every_up, preferred_element_type=jnp.float32
    )
    gathered_output = widened_output.astype(jnp.bfloat16).reshape(
        adapter_count * capacity, output_columns
    )
    adapter_output = gathered_output[destination_rows]
    total_output = base_output + adapter_output.astype(jnp.float32)
    return jnp.where(alive_mask[:, None], total_output, 0.0).astype(jnp.bfloat16)


def solution(mesh):
    in_specs = (
        P(("group", "replica"), "tensor"),
        P(("group", "replica"), None),
        P("group"),
        P(("group", "replica")),
        P("tensor", None),
        P(("group", "replica"), None, "tensor"),
        P(("group", "replica"), None, "tensor"),
    )
    out_specs = P(("group", "replica"), "tensor")
    return jax.shard_map(shards, mesh=mesh, in_specs=in_specs, out_specs=out_specs, check_vma=False)
```

profile of v0, /device:TPU:0, one launch (start us, length us, event | category | flops | bytes accessed | tf_op | source)
XLA Modules:
  0.0 624.8 jit_solution(2044897595741382759)
XLA Ops:
  6.5 0.0 all-gather.5.cloned.1.call-start
  6.5 0.7 all-gather.5.cloned.1.call-update
  7.3 0.0 all-gather.3.cloned.1.call-start
  7.3 0.7 all-gather.3.cloned.1.call-update
  8.0 0.8 select_reduce_fusion
  8.8 9.0 %reduce-window.6 = s32[32,8,128]{2,1,0:T(8,128)S(1)} reduce-window(s32[32,8,128]{2,1,0:T(8,128)S(1)} %fusion.3, s32[]{:T(128)} %constant.6.clone.1), window={size=1x1x128 pad=0_0x0_0x127_0}, to_apply=%region_1.2 | reduce-window | flops 4161536 | bytes 262148 | tf_op jit(solution)/shard_map/reduce-window
  17.8 0.1 slice.10
  17.9 0.1 copy.10
  18.1 0.1 copy.11
  18.9 0.1 broadcast_add_fusion
  19.0 14.1 %broadcast_select_fusion = bf16[1024,8192]{1,0:T(8,128)(2,1)} fusion(bf16[1024,8192]{1,0:T(8,128)(2,1)} %param.7, pred[1024]{0:T(1024)(128)(4,1)S(1)} %iota_compare_fusion.3), kind=kLoop, calls=%fused_computation.2 | loop fusion | flops 8388608 | bytes 33555456 | tf_op jit(solution)/shard_map/jit(_where)/select_n | solution.py:32
  33.1 11.0 %broadcast_in_dim.47 = bf16[2048,8192]{1,0:T(8,128)(2,1)} broadcast(bf16[]{:T(256)} %constant.5.clone.1), dimensions={} | broadcast | bytes 33554432 | tf_op jit(solution)/shard_map/broadcast_in_dim | solution.py:34
  44.1 514.1 %scatter_fusion = bf16[2048,8192]{1,0:T(8,128)(2,1)} fusion(bf16[2048,8192]{1,0:T(8,128)(2,1)} %broadcast_in_dim.47, s32[1024]{0:T(1024)S(1)} %bitcast.35, bf16[1024,8192]{1,0:T(8,128)(2,1)} %broadcast_select_fusion), kind=kCustom, calls=%fused_computation.1 | custom fusion | bytes 50335744 | tf_op jit(solution)/shard_map/scatter | solution.py:36
  558.3 0.0 all-gather.5.cloned.1.call-done
  558.3 0.0 all-gather.3.cloned.1.call-done
  558.3 26.1 %convolution_convert_fusion = bf16[32,64,1024]{2,1,0:T(8,128)(2,1)} fusion(bf16[32,64,1024]{2,1,0:T(8,128)(2,1)} %all-gather.5.cloned.1.call-done, bf16[32,64,8192]{2,1,0:T(8,128)(2,1)} %bitcast.31, bf16[32,64,8192]{2,1,0:T(8,128)(2,1)} %all-gather.3.cloned.1.call-done), kind=kOutput, calls=%fused_computation.4 | convolution fusion | flops 2418147328 | bytes 75497472 | tf_op jit(solution)/shard_map/acr,are->ace/dot_general | solution.py:47
  584.4 7.7 %gather_fusion = bf16[1024,1024]{1,0:T(8,128)(2,1)S(1)} fusion(bf16[2048,1024]{1,0:T(8,128)(2,1)} %bitcast.32, s32[1024]{0:T(1024)S(1)} %broadcast_clamp_fusion), kind=kCustom, calls=%fused_computation | custom fusion | bytes 4198400 | tf_op jit(solution)/shard_map/gather | solution.py:53
  592.1 25.9 %select_convert_fusion = bf16[1024,1024]{1,0:T(8,128)(2,1)} fusion(bf16[1024,1024]{1,0:T(8,128)(2,1)S(1)} %gather_fusion, bf16[1024,8192]{1,0:T(8,128)(2,1)} %param.7, bf16[8192,1024]{1,0:T(8,128)(2,1)} %param.11, pred[1024]{0:T(1024)(128)(4,1)S(1)} %iota_compare_fusion.3), kind=kOutput, calls=%fused_computation.3 | convolution fusion | flops 17184063488 | bytes 37749760 | tf_op jit(solution)/shard_map/dot_general | solution.py:30
  (8 shorter events, 0.1 us)
Async XLA Ops:
  6.5 551.7 %all-gather.5.cloned.1.call-start = ((), (), s32[]{:S(2)}) async-start(), calls=%async_computation.1 | async-start | bytes 4456448 | tf_op jit(solution)/shard_map/all_gather | solution.py:40
  7.3 551.0 %all-gather.3.cloned.1.call-start = ((), (), s32[]{:S(2)}) async-start(), calls=%async_computation | async-start | bytes 35651584 | tf_op jit(solution)/shard_map/all_gather | solution.py:39
Sparse Core Ops, SparseCore 0:
  9.5 53.4 all-gather.4
  64.6 166.5 all-gather.2
where the time goes:
time: 630 us; the launch traced here: 625 us
  local copies, waits for them, and re-layouts  533 us (85%)
  matrix products  52 us (8%)
  other arithmetic  24.1 us (4%)
  between operations  14.1 us (2%)
    scatter x1, local copies, waits for them, and re-layouts, shards(): buffer = jnp.zeros((adapter_count * capacity, feat_cols), jnp.bfloat16).a...  514 us
    dot_general x1, matrix products, shards(): jnp.einsum('acr,are->ace', reduced_rows, every_up, preferred_element_type...  26.1 us
    dot_general x1, matrix products, shards(): jnp.dot(tokens, value_weight, preferred_element_type=jnp.float32)  25.9 us
    select_n x1, other arithmetic, shards(): sending = jnp.where(alive_mask[:, None], tokens, jnp.zeros_like(tokens))  14.1 us
  transfers between devices with their start and end apart: 2, of which 0 were waited for; matrix products, arithmetic and copies ran while one was open for 88% of the time, Pallas kernels for 0%

commit v1 on v0

v1 whole, which is shorter than its diff:
```python
import functools

import jax
import jax.numpy as jnp
from jax import lax
from jax.experimental import pallas as pl
from jax.experimental.pallas import tpu as pltpu
from jax.sharding import PartitionSpec as P

MESH = pl.DeviceIdType.MESH
CHUNK_ROWS = 16
BASE_DEPTH = 1024
SHRINK_DEPTH = 1024
TILE = 256


def gather_kernel(
    replicas,
    rank,
    tok_hbm,
    weight_hbm,
    down_hbm,
    up_hbm,
    ident_ref,
    place_ref,
    out_ref,
    every_down,
    every_up,
    tok,
    weight,
    down,
    up,
    slot,
    total,
    shrunk,
    tok_sem,
    weight_sem,
    load_sem,
    ring_send,
    ring_recv,
    pair_send,
    pair_recv,
):
    rows, width = tok.shape
    features = total.shape[1]
    chips = replicas // 2
    half = chips // 2
    chunks = rank // CHUNK_ROWS
    parts = chunks + 1
    base_steps = width // BASE_DEPTH

    me = lax.axis_index("replica")
    core = lax.rem(me, 2)
    chip = me // 2
    column, level = lax.rem(chip, 2), chip // 2
    here = level + column * (chips - 1 - 2 * level)

    def replica_at(place, core_at):
        second = place // half
        level_at = place + second * (chips - 1 - 2 * place)
        return (level_at * 2 + second) * 2 + core_at

    right = replica_at(lax.rem(here + 1, chips), core)
    left = replica_at(lax.rem(here + chips - 1, chips), core)
    sibling = me + 1 - 2 * core

    def owner_slot(step, way, core_at):
        place = lax.rem(here + chips - step + 2 * way * step, chips)
        return replica_at(place, core_at) * 2 + way

    def piece(slot_at, part):
        if part == chunks:
            return every_up.at[slot_at]
        return every_down.at[slot_at, pl.ds(part * CHUNK_ROWS, CHUNK_ROWS)]

    def own_piece(way, part):
        if part == chunks:
            return up_hbm.at[way]
        return down_hbm.at[way, pl.ds(part * CHUNK_ROWS, CHUNK_ROWS)]

    def ring(step, way, part, src):
        at = ((step - 1) * 2 + way) * parts + part
        return pltpu.make_async_remote_copy(
            src_ref=src,
            dst_ref=piece(owner_slot(step - 1, way, core), part),
            send_sem=ring_send.at[at],
            recv_sem=ring_recv.at[at],
            device_id={"replica": left if way else right},
            device_id_type=MESH,
        )

    def ring_arrival(step, way, part):
        at = ((step - 1) * 2 + way) * parts + part
        ref = piece(owner_slot(step, way, core), part)
        return pltpu.make_async_remote_copy(
            src_ref=ref,
            dst_ref=ref,
            send_sem=ring_send.at[at],
            recv_sem=ring_recv.at[at],
            device_id={"replica": right if way else left},
            device_id_type=MESH,
        )

    def pair(step, way, part, src, core_at):
        at = (step * 2 + way) * parts + part
        return pltpu.make_async_remote_copy(
            src_ref=src,
            dst_ref=piece(owner_slot(step, way, core_at), part),
            send_sem=pair_send.at[at],
            recv_sem=pair_recv.at[at],
            device_id={"replica": sibling},
            device_id_type=MESH,
        )

    def tok_load(k):
        cols = pl.ds(pl.multiple_of(k * BASE_DEPTH, BASE_DEPTH), BASE_DEPTH)
        return pltpu.make_async_copy(tok_hbm.at[:, cols], tok.at[:, cols], tok_sem.at[k])

    def weight_load(k):
        depth = pl.ds(pl.multiple_of(k * BASE_DEPTH, BASE_DEPTH), BASE_DEPTH)
        return pltpu.make_async_copy(
            weight_hbm.at[depth], weight.at[lax.rem(k, 2)], weight_sem.at[lax.rem(k, 2)]
        )

    order = [*range(chunks), chunks]

    barrier = pltpu.get_barrier_semaphore()
    for other in (left, right, sibling):
        pl.semaphore_signal(barrier, inc=1, device_id={"replica": other}, device_id_type=MESH)
    pl.semaphore_wait(barrier, 3)

    for part in order:
        for way in range(2):
            ring(1, way, part, own_piece(way, part)).start()
    for part in order:
        for way in range(2):
            pair(0, way, part, own_piece(way, part), core).start()

    weight_load(0).start()
    for k in range(base_steps):
        tok_load(k).start()

    named = ident_ref[...] == lax.broadcasted_iota(jnp.int32, (rows, place_ref.shape[1]), 1)
    slot[...] = jnp.sum(jnp.where(named, place_ref[...], 0), axis=1, keepdims=True)
    total[...] = jnp.zeros_like(total)

    @pl.loop(0, base_steps)
    def _(k):
        @pl.when(k + 1 < base_steps)
        def _():
            weight_load(k + 1).start()

        tok_load(k).wait()
        weight_load(k).wait()
        depth = pl.ds(pl.multiple_of(k * BASE_DEPTH, BASE_DEPTH), BASE_DEPTH)

        @pl.loop(0, features // TILE)
        def _(j):
            cols = pl.ds(pl.multiple_of(j * TILE, TILE), TILE)
            total[:, cols] += jnp.dot(
                tok[:, depth],
                weight[lax.rem(k, 2), :, cols],
                preferred_element_type=jnp.float32,
            )

    def loads(step, own):
        at = lax.rem(step, 2)
        copies = []
        for quarter in range(4):
            way = quarter % 2
            spot = pl.ds(quarter * rank, rank)
            if own and quarter < 2:
                sources = down_hbm.at[way], up_hbm.at[way]
            else:
                whose = core if quarter < 2 else 1 - core
                where = owner_slot(step, way, whose)
                sources = every_down.at[where], every_up.at[where]
            copies.append(
                pltpu.make_async_copy(sources[0], down.at[at, spot], load_sem.at[at, quarter, 0])
            )
            copies.append(
                pltpu.make_async_copy(sources[1], up.at[at, spot], load_sem.at[at, quarter, 1])
            )
        return copies

    def pair_arrivals(step):
        for part in order:
            for way in range(2):
                ref = piece(owner_slot(step, way, 1 - core), part)
                pair(step, way, part, ref, 1 - core).wait_recv()

    def apply(step):
        at = lax.rem(step, 2)
        for copy in loads(step, False):
            copy.wait()
        shrunk[...] = jnp.zeros_like(shrunk)

        @pl.loop(0, width // SHRINK_DEPTH)
        def _(k):
            depth = pl.ds(pl.multiple_of(k * SHRINK_DEPTH, SHRINK_DEPTH), SHRINK_DEPTH)
            shrunk[...] += lax.dot_general(
                tok[:, depth],
                down[at, :, depth],
                (((1,), (1,)), ((), ())),
                preferred_element_type=jnp.float32,
            )

        lane = lax.broadcasted_iota(jnp.int32, (1, 4 * rank), 1)
        lane_slot = owner_slot(step, 1, 1 - core)
        for quarter in (2, 1, 0):
            whose = core if quarter < 2 else 1 - core
            lane_slot = jnp.where(
                lane < (quarter + 1) * rank, owner_slot(step, quarter % 2, whose), lane_slot
            )

        @pl.loop(0, rows // TILE)
        def _(i):
            spot = pl.ds(pl.multiple_of(i * TILE, TILE), TILE)
            chosen = jnp.where(slot[spot] == lane_slot, shrunk[spot], 0.0).astype(jnp.bfloat16)
            delta = jnp.dot(chosen, up[at], preferred_element_type=jnp.float32)
            total[spot] += delta.astype(jnp.bfloat16).astype(jnp.float32)

    pair_arrivals(0)
    for copy in loads(0, True):
        copy.start()

    @pl.loop(1, chips)
    def _(step):
        apply(step - 1)
        for part in order:
            for way in range(2):
                ring_arrival(step, way, part).wait_recv()
                ref = piece(owner_slot(step, way, core), part)

                @pl.when(step + 1 < chips)
                def _():
                    ring(step + 1, way, part, ref).start()

                pair(step, way, part, ref, core).start()
        pair_arrivals(step)
        for copy in loads(step, False):
            copy.start()

    apply(chips - 1)
    out_ref[...] = total[...].astype(jnp.bfloat16)

    for part in order:
        for way in range(2):
            ring(1, way, part, own_piece(way, part)).wait_send()
            pair(0, way, part, own_piece(way, part), core).wait_send()

    @pl.loop(1, chips)
    def _(step):
        for part in order:
            for way in range(2):
                ref = piece(owner_slot(step, way, core), part)

                @pl.when(step + 1 < chips)
                def _():
                    ring(step + 1, way, part, ref).wait_send()

                pair(step, way, part, ref, core).wait_send()


def ring_shards(
    replicas,
    tokens,
    token_adapter,
    adapter_position,
    replica_live_rows,
    value_weight,
    adapter_down_weight,
    adapter_up_weight,
):
    rows, width = tokens.shape
    owned, rank, features = adapter_up_weight.shape
    adapters = adapter_position.shape[0]
    chips = replicas // 2
    parts = rank // CHUNK_ROWS + 1
    any_space = pl.BlockSpec(memory_space=pl.ANY)
    vmem = pl.BlockSpec(memory_space=pltpu.VMEM)
    dma = pltpu.SemaphoreType.DMA
    values, _, _ = pl.pallas_call(
        functools.partial(gather_kernel, replicas, rank),
        out_shape=(
            jax.ShapeDtypeStruct((rows, features), jnp.bfloat16),
            jax.ShapeDtypeStruct((adapters, rank, width), jnp.bfloat16),
            jax.ShapeDtypeStruct((adapters, rank, features), jnp.bfloat16),
        ),
        in_specs=[any_space] * 4 + [vmem] * 2,
        out_specs=(vmem, any_space, any_space),
        scratch_shapes=[
            pltpu.VMEM((rows, width), jnp.bfloat16),
            pltpu.VMEM((2, BASE_DEPTH, features), jnp.bfloat16),
            pltpu.VMEM((2, 4 * rank, width), jnp.bfloat16),
            pltpu.VMEM((2, 4 * rank, features), jnp.bfloat16),
            pltpu.VMEM((rows, 1), jnp.int32),
            pltpu.VMEM((rows, features), jnp.float32),
            pltpu.VMEM((rows, 4 * rank), jnp.float32),
            dma((width // BASE_DEPTH,)),
            dma((2,)),
            dma((2, 4, 2)),
            dma(((chips - 1) * 2 * parts,)),
            dma(((chips - 1) * 2 * parts,)),
            dma((chips * 2 * parts,)),
            dma((chips * 2 * parts,)),
        ],
        compiler_params=pltpu.CompilerParams(
            collective_id=0, has_side_effects=True, vmem_limit_bytes=52 * 2**20
        ),
        cost_estimate=pl.CostEstimate(
            flops=2 * rows * width * (features + adapters * rank)
            + 2 * rows * features * adapters * rank,
            bytes_accessed=2 * (rows * width + width * features + 3 * adapters * rank * width),
            transcendentals=0,
        ),
        name="gather_and_project",
    )(
        tokens,
        value_weight,
        adapter_down_weight,
        adapter_up_weight,
        token_adapter,
        adapter_position[None, :],
    )
    alive = jnp.arange(rows, dtype=jnp.int32) < replica_live_rows[0]
    return jnp.where(alive[:, None], values, jnp.zeros_like(values))


def split_shards(
    tokens,
    token_adapter,
    adapter_position,
    replica_live_rows,
    value_weight,
    adapter_down_weight,
    adapter_up_weight,
):
    rows = tokens.shape[0]
    adapters = adapter_position.shape[0]
    rank = adapter_up_weight.shape[1]
    every_down = lax.all_gather(adapter_down_weight, "replica", axis=0, tiled=True)
    every_up = lax.all_gather(adapter_up_weight, "replica", axis=0, tiled=True)
    base = lax.psum_scatter(
        jnp.dot(tokens, value_weight, preferred_element_type=jnp.float32),
        "tensor",
        scatter_dimension=1,
        tiled=True,
    )
    ids = jnp.arange(adapters, dtype=jnp.int32)[None, :]
    slot = jnp.sum(jnp.where(token_adapter == ids, adapter_position[None, :], 0), axis=1)
    hot = slot[:, None] == ids
    partial = jnp.einsum("td,ard->tar", tokens, every_down, preferred_element_type=jnp.float32)
    partial = jnp.sum(jnp.where(hot[:, :, None], partial, 0.0), axis=1)
    shrunk = lax.psum(partial, "tensor").astype(jnp.bfloat16)
    spread = jnp.where(hot[:, :, None], shrunk[:, None, :], jnp.zeros((), jnp.bfloat16))
    delta = jnp.dot(
        spread.reshape(rows, adapters * rank),
        every_up.reshape(adapters * rank, -1),
        preferred_element_type=jnp.float32,
    ).astype(jnp.bfloat16)
    alive = jnp.arange(rows, dtype=jnp.int32) < replica_live_rows[0]
    return jnp.where(alive[:, None], base + delta.astype(jnp.float32), 0.0).astype(jnp.bfloat16)


def solution(mesh):
    in_specs = (
        P(("group", "replica"), "tensor"),
        P(("group", "replica"), None),
        P("group"),
        P(("group", "replica")),
        P("tensor", None),
        P(("group", "replica"), None, "tensor"),
        P(("group", "replica"), None, "tensor"),
    )
    out_specs = P(("group", "replica"), "tensor")
    if mesh.shape["tensor"] == 1:
        body = functools.partial(ring_shards, mesh.shape["replica"])
    else:
        body = split_shards
    return jax.shard_map(body, mesh=mesh, in_specs=in_specs, out_specs=out_specs, check_vma=False)
```

time: 630 us -> 219 us (0.35)
  local copies, waits for them, and re-layouts: 533 us -> 2.5 us
  Pallas kernels: 0 us -> 211 us
  matrix products: 52 us -> 0 us
  other arithmetic: 24.1 us -> 3.14 us
  between operations: 14.1 us -> 0.68 us
    scatter x1 -> x0, local copies, waits for them, and re-layouts: 514 us -> none  [shards(): buffer = jnp.zeros((adapter_count * capacity, feat_cols), jnp.bfloat16).a...]
    pallas_call x0 -> x1, Pallas kernels: none -> 211 us  [ring_shards(): pl.pallas_call(functools.partial(gather_kernel, replicas, rank), out_shap...]
    dot_general x2 -> x0, matrix products: 52 us -> none  [the longest x1 26.1 us: shards(): jnp.einsum('acr,are->ace', reduced_rows, every_up, preferred_element_type...]
    broadcast_in_dim x1 -> x0, local copies, waits for them, and re-layouts: 11 us -> none  [shards(): jnp.zeros((adapter_count * capacity, feat_cols), jnp.bfloat16)]
    select_n x2 -> x1, other arithmetic: 14.1 us -> 3.13 us  [ring_shards(): return jnp.where(alive[:, None], values, jnp.zeros_like(values))]
    another operation x3 -> x0, other arithmetic: 9.14 us -> none
    gather x1 -> x0, local copies, waits for them, and re-layouts: 7.7 us -> none  [shards(): adapter_output = gathered_output[destination_rows]]
  transfers between devices with their start and end apart: 2 -> 0, of which waited for: 0 -> 0; matrix products, arithmetic and copies ran while one was open for 88% -> 0% of each run, Pallas kernels for 0% -> 0%
where the time goes in v1:
time: 219 us; the launch traced here: 217 us
  Pallas kernels  211 us (96%)
  other arithmetic  3.14 us (1%)
  local copies, waits for them, and re-layouts  2.5 us (1%)
    pallas_call x1, Pallas kernels, ring_shards(): pl.pallas_call(functools.partial(gather_kernel, replicas, rank), out_shap...  211 us

profile of v1, /device:TPU:0, one launch (start us, length us, event | category | flops | bytes accessed | tf_op | source)
XLA Modules:
  0.0 217.5 jit_solution(470771143421225274)
XLA Ops:
  0.0 0.9 copy.8.ident_ref
  0.9 0.0 copy-start
  0.9 0.9 copy-done
  1.9 0.0 copy-start.1
  1.9 0.7 copy-done.1
  2.5 211.2 %gather_and_project.1 = (bf16[1024,1024]{1,0:T(8,128)(2,1)}, bf16[32,64,8192]{2,1,0:T(8,128)(2,1)}, bf16[32,64,1024]{2,1,0:T(8,128)(2,1)}) custom-call(bf16[1024,8192]{1,0:T(8,128)(2,1)} %tok_hbm.1, bf16[8192,1024]{1,0:T(8,128)(2,1)} %weight_hbm.1, bf16[2,64,8192]{2,1,0:T(8,128)(2,1)} %down_hbm.1, bf16[2,64,1024]{2,1,0:T(8,128)(2,1)S(1)} %copy-done, ...), custom_call_target="tpu_custom_call" | custom-call | flops 55834574848 | bytes 134217728 | tf_op jit(solution)/shard_map/gather_and_project/pallas_call | solution.py:283
  214.4 3.1 %broadcast_select_fusion = bf16[1024,1024]{1,0:T(8,128)(2,1)} fusion(bf16[1024,1024]{1,0:T(8,128)(2,1)} %get-tuple-element.6, pred[1024]{0:T(1024)(128)(4,1)S(1)} %iota_compare_fusion), kind=kLoop, calls=%fused_computation | loop fusion | flops 1048576 | bytes 4195328 | tf_op jit(solution)/shard_map/jit(_where)/select_n | solution.py:327
  (1 shorter events, 0.0 us)
Async XLA Ops:
  0.9 1.0 copy-start
  1.9 0.7 copy-start.1

commit v2 on v1

--- a/solution.py
+++ b/solution.py
@@ -8,9 +8,8 @@
 from jax.sharding import PartitionSpec as P
 
 MESH = pl.DeviceIdType.MESH
-CHUNK_ROWS = 16
+CHUNKS = 4
 BASE_DEPTH = 1024
-SHRINK_DEPTH = 1024
 TILE = 256
 
 
@@ -45,9 +44,11 @@
     features = total.shape[1]
     chips = replicas // 2
     half = chips // 2
-    chunks = rank // CHUNK_ROWS
+    chunks = CHUNKS
     parts = chunks + 1
+    span = width // chunks
     base_steps = width // BASE_DEPTH
+    last = (chips - 1) * chunks - 1
 
     me = lax.axis_index("replica")
     core = lax.rem(me, 2)
@@ -68,15 +69,18 @@
         place = lax.rem(here + chips - step + 2 * way * step, chips)
         return replica_at(place, core_at) * 2 + way
 
+    def span_of(part):
+        return pl.ds(pl.multiple_of(part * span, span), span)
+
     def piece(slot_at, part):
-        if part == chunks:
+        if isinstance(part, int) and part == chunks:
             return every_up.at[slot_at]
-        return every_down.at[slot_at, pl.ds(part * CHUNK_ROWS, CHUNK_ROWS)]
+        return every_down.at[slot_at, :, span_of(part)]
 
     def own_piece(way, part):
-        if part == chunks:
+        if isinstance(part, int) and part == chunks:
             return up_hbm.at[way]
-        return down_hbm.at[way, pl.ds(part * CHUNK_ROWS, CHUNK_ROWS)]
+        return down_hbm.at[way, :, span_of(part)]
 
     def ring(step, way, part, src):
         at = ((step - 1) * 2 + way) * parts + part
@@ -113,7 +117,7 @@
         )
 
     def tok_load(k):
-        cols = pl.ds(pl.multiple_of(k * BASE_DEPTH, BASE_DEPTH), BASE_DEPTH)
+        cols = span_of(k)
         return pltpu.make_async_copy(tok_hbm.at[:, cols], tok.at[:, cols], tok_sem.at[k])
 
     def weight_load(k):
@@ -122,7 +126,7 @@
             weight_hbm.at[depth], weight.at[lax.rem(k, 2)], weight_sem.at[lax.rem(k, 2)]
         )
 
-    order = [*range(chunks), chunks]
+    order = [chunks, *range(chunks)]
 
     barrier = pltpu.get_barrier_semaphore()
     for other in (left, right, sibling):
@@ -136,21 +140,16 @@
         for way in range(2):
             pair(0, way, part, own_piece(way, part), core).start()
 
+    for k in range(chunks):
+        tok_load(k).start()
     weight_load(0).start()
-    for k in range(base_steps):
-        tok_load(k).start()
+    weight_load(1).start()
 
     named = ident_ref[...] == lax.broadcasted_iota(jnp.int32, (rows, place_ref.shape[1]), 1)
     slot[...] = jnp.sum(jnp.where(named, place_ref[...], 0), axis=1, keepdims=True)
     total[...] = jnp.zeros_like(total)
 
-    @pl.loop(0, base_steps)
-    def _(k):
-        @pl.when(k + 1 < base_steps)
-        def _():
-            weight_load(k + 1).start()
-
-        tok_load(k).wait()
+    def base(k):
         weight_load(k).wait()
         depth = pl.ds(pl.multiple_of(k * BASE_DEPTH, BASE_DEPTH), BASE_DEPTH)
 
@@ -163,86 +162,140 @@
                 preferred_element_type=jnp.float32,
             )
 
-    def loads(step, own):
-        at = lax.rem(step, 2)
-        copies = []
+        @pl.when(k + 2 < base_steps)
+        def _():
+            weight_load(k + 2).start()
+
+    def whose(quarter):
+        return core if quarter < 2 else 1 - core
+
+    def down_load(step, k, quarter, own=False):
+        way = quarter % 2
+        src = own_piece(way, k) if own else piece(owner_slot(step, way, whose(quarter)), k)
+        return pltpu.make_async_copy(
+            src, down.at[pl.ds(quarter * rank, rank)], load_sem.at[quarter, 0]
+        )
+
+    def up_load(step, quarter, own=False):
+        way = quarter % 2
+        src = up_hbm.at[way] if own else every_up.at[owner_slot(step, way, whose(quarter))]
+        return pltpu.make_async_copy(
+            src, up.at[pl.ds(quarter * rank, rank)], load_sem.at[quarter, 1]
+        )
+
+    def arrive(step, part):
+        for way in range(2):
+            ring_arrival(step, way, part).wait_recv()
+            ref = piece(owner_slot(step, way, core), part)
+
+            @pl.when(step + 1 < chips)
+            def _():
+                ring(step + 1, way, part, ref).start()
+
+            pair(step, way, part, ref, core).start()
+
+    def pair_arrive(step, part):
+        for way in range(2):
+            ref = piece(owner_slot(step, way, 1 - core), part)
+            pair(step, way, part, ref, 1 - core).wait_recv()
+
+    def fetch(step, k, own=False):
+        for quarter in range(2):
+            down_load(step, k, quarter, own).start()
+
+        @pl.when(k == 0)
+        def _():
+            for quarter in range(2):
+                up_load(step, quarter, own).start()
+            pair_arrive(step, chunks)
+            for quarter in range(2, 4):
+                up_load(step, quarter).start()
+
+        pair_arrive(step, k)
+        for quarter in range(2, 4):
+            down_load(step, k, quarter).start()
+
+    def shrink(step, k):
         for quarter in range(4):
-            way = quarter % 2
-            spot = pl.ds(quarter * rank, rank)
-            if own and quarter < 2:
-                sources = down_hbm.at[way], up_hbm.at[way]
-            else:
-                whose = core if quarter < 2 else 1 - core
-                where = owner_slot(step, way, whose)
-                sources = every_down.at[where], every_up.at[where]
-            copies.append(
-                pltpu.make_async_copy(sources[0], down.at[at, spot], load_sem.at[at, quarter, 0])
-            )
-            copies.append(
-                pltpu.make_async_copy(sources[1], up.at[at, spot], load_sem.at[at, quarter, 1])
-            )
-        return copies
-
-    def pair_arrivals(step):
-        for part in order:
-            for way in range(2):
-                ref = piece(owner_slot(step, way, 1 - core), part)
-                pair(step, way, part, ref, 1 - core).wait_recv()
-
-    def apply(step):
-        at = lax.rem(step, 2)
-        for copy in loads(step, False):
-            copy.wait()
-        shrunk[...] = jnp.zeros_like(shrunk)
-
-        @pl.loop(0, width // SHRINK_DEPTH)
-        def _(k):
-            depth = pl.ds(pl.multiple_of(k * SHRINK_DEPTH, SHRINK_DEPTH), SHRINK_DEPTH)
-            shrunk[...] += lax.dot_general(
-                tok[:, depth],
-                down[at, :, depth],
+            down_load(step, k, quarter).wait()
+
+        def product():
+            return lax.dot_general(
+                tok[:, span_of(k)],
+                down[...],
                 (((1,), (1,)), ((), ())),
                 preferred_element_type=jnp.float32,
             )
 
+        @pl.when(k == 0)
+        def _():
+            shrunk[...] = jnp.zeros_like(shrunk)
+
+        shrunk[...] += product()
+
+    def widen(step, store):
+        for quarter in range(4):
+            up_load(step, quarter).wait()
         lane = lax.broadcasted_iota(jnp.int32, (1, 4 * rank), 1)
         lane_slot = owner_slot(step, 1, 1 - core)
         for quarter in (2, 1, 0):
-            whose = core if quarter < 2 else 1 - core
             lane_slot = jnp.where(
-                lane < (quarter + 1) * rank, owner_slot(step, quarter % 2, whose), lane_slot
+                lane < (quarter + 1) * rank,
+                owner_slot(step, quarter % 2, whose(quarter)),
+                lane_slot,
             )
 
         @pl.loop(0, rows // TILE)
         def _(i):
             spot = pl.ds(pl.multiple_of(i * TILE, TILE), TILE)
             chosen = jnp.where(slot[spot] == lane_slot, shrunk[spot], 0.0).astype(jnp.bfloat16)
-            delta = jnp.dot(chosen, up[at], preferred_element_type=jnp.float32)
-            total[spot] += delta.astype(jnp.bfloat16).astype(jnp.float32)
-
-    pair_arrivals(0)
-    for copy in loads(0, True):
-        copy.start()
-
-    @pl.loop(1, chips)
-    def _(step):
-        apply(step - 1)
-        for part in order:
-            for way in range(2):
-                ring_arrival(step, way, part).wait_recv()
-                ref = piece(owner_slot(step, way, core), part)
-
-                @pl.when(step + 1 < chips)
-                def _():
-                    ring(step + 1, way, part, ref).start()
-
-                pair(step, way, part, ref, core).start()
-        pair_arrivals(step)
-        for copy in loads(step, False):
-            copy.start()
-
-    apply(chips - 1)
-    out_ref[...] = total[...].astype(jnp.bfloat16)
+            delta = jnp.dot(chosen, up[...], preferred_element_type=jnp.float32)
+            result = total[spot] + delta.astype(jnp.bfloat16).astype(jnp.float32)
+            if store:
+                out_ref[spot] = result.astype(jnp.bfloat16)
+            else:
+                total[spot] = result
+
+    def apply(step, k):
+        shrink(step, k)
+
+        @pl.when(k == chunks - 1)
+        def _():
+            widen(step, False)
+
+    @pl.loop(0, chunks)
+    def _(k):
+        tok_load(k).wait()
+        fetch(0, k, True)
+        apply(0, k)
+
+    @pl.loop(0, last + 1)
+    def _(unit):
+        step, k = unit // chunks + 1, lax.rem(unit, chunks)
+        before, before_k = (unit - 1) // chunks + 1, lax.rem(unit + chunks - 1, chunks)
+
+        @pl.when(unit == last)
+        def _():
+            apply(before, before_k)
+
+        @pl.when(k == 0)
+        def _():
+            arrive(step, chunks)
+
+        arrive(step, k)
+
+        @pl.when(unit * (last - unit) > 0)
+        def _():
+            apply(before, before_k)
+
+        fetch(step, k)
+
+        @pl.when(unit < base_steps)
+        def _():
+            base(unit)
+
+    shrink(chips - 1, chunks - 1)
+    widen(chips - 1, True)
 
     for part in order:
         for way in range(2):
@@ -276,7 +329,7 @@
     owned, rank, features = adapter_up_weight.shape
     adapters = adapter_position.shape[0]
     chips = replicas // 2
-    parts = rank // CHUNK_ROWS + 1
+    parts = CHUNKS + 1
     any_space = pl.BlockSpec(memory_space=pl.ANY)
     vmem = pl.BlockSpec(memory_space=pltpu.VMEM)
     dma = pltpu.SemaphoreType.DMA
@@ -292,14 +345,14 @@
         scratch_shapes=[
             pltpu.VMEM((rows, width), jnp.bfloat16),
             pltpu.VMEM((2, BASE_DEPTH, features), jnp.bfloat16),
-            pltpu.VMEM((2, 4 * rank, width), jnp.bfloat16),
-            pltpu.VMEM((2, 4 * rank, features), jnp.bfloat16),
+            pltpu.VMEM((4 * rank, width // CHUNKS), jnp.bfloat16),
+            pltpu.VMEM((4 * rank, features), jnp.bfloat16),
             pltpu.VMEM((rows, 1), jnp.int32),
             pltpu.VMEM((rows, features), jnp.float32),
             pltpu.VMEM((rows, 4 * rank), jnp.float32),
-            dma((width // BASE_DEPTH,)),
+            dma((CHUNKS,)),
             dma((2,)),
-            dma((2, 4, 2)),
+            dma((4, 2)),
             dma(((chips - 1) * 2 * parts,)),
             dma(((chips - 1) * 2 * parts,)),
             dma((chips * 2 * parts,)),

time: 219 us -> 199 us (0.909)
  Pallas kernels: 211 us -> 192 us
    pallas_call x1, Pallas kernels: 211 us -> 192 us  [ring_shards(): pl.pallas_call(functools.partial(gather_kernel, replicas, rank), out_shap...]
where the time goes in v2:
time: 199 us; the launch traced here: 198 us
  Pallas kernels  192 us (96%)
  other arithmetic  3.14 us (2%)
  local copies, waits for them, and re-layouts  2.5 us (1%)
    pallas_call x1, Pallas kernels, ring_shards(): pl.pallas_call(functools.partial(gather_kernel, replicas, rank), out_shap...  192 us

profile of v2, /device:TPU:0, one launch (start us, length us, event | category | flops | bytes accessed | tf_op | source)
XLA Modules:
  0.0 198.3 jit_solution(9873506603108260921)
XLA Ops:
  0.0 0.9 copy.8.ident_ref
  0.9 0.0 copy-start
  0.9 0.9 copy-done
  1.9 0.0 copy-start.1
  1.9 0.7 copy-done.1
  2.5 191.9 %gather_and_project.1 = (bf16[1024,1024]{1,0:T(8,128)(2,1)}, bf16[32,64,8192]{2,1,0:T(8,128)(2,1)}, bf16[32,64,1024]{2,1,0:T(8,128)(2,1)}) custom-call(bf16[1024,8192]{1,0:T(8,128)(2,1)} %tok_hbm.1, bf16[8192,1024]{1,0:T(8,128)(2,1)} %weight_hbm.1, bf16[2,64,8192]{2,1,0:T(8,128)(2,1)} %down_hbm.1, bf16[2,64,1024]{2,1,0:T(8,128)(2,1)S(1)} %copy-done, ...), custom_call_target="tpu_custom_call" | custom-call | flops 55834574848 | bytes 134217728 | tf_op jit(solution)/shard_map/gather_and_project/pallas_call | solution.py:336
  195.1 3.1 %broadcast_select_fusion = bf16[1024,1024]{1,0:T(8,128)(2,1)} fusion(bf16[1024,1024]{1,0:T(8,128)(2,1)} %get-tuple-element.6, pred[1024]{0:T(1024)(128)(4,1)S(1)} %iota_compare_fusion), kind=kLoop, calls=%fused_computation | loop fusion | flops 1048576 | bytes 4195328 | tf_op jit(solution)/shard_map/jit(_where)/select_n | solution.py:380
  (1 shorter events, 0.0 us)
Async XLA Ops:
  0.9 1.0 copy-start
  1.9 0.7 copy-start.1

commit v3 on v2

--- a/solution.py
+++ b/solution.py
@@ -11,6 +11,7 @@
 CHUNKS = 4
 BASE_DEPTH = 1024
 TILE = 256
+LANES = 128
 
 
 def gather_kernel(
@@ -20,8 +21,7 @@
     weight_hbm,
     down_hbm,
     up_hbm,
-    ident_ref,
-    place_ref,
+    slot_ref,
     out_ref,
     every_down,
     every_up,
@@ -145,8 +145,14 @@
     weight_load(0).start()
     weight_load(1).start()
 
-    named = ident_ref[...] == lax.broadcasted_iota(jnp.int32, (rows, place_ref.shape[1]), 1)
-    slot[...] = jnp.sum(jnp.where(named, place_ref[...], 0), axis=1, keepdims=True)
+    diagonal = lax.broadcasted_iota(jnp.int32, (LANES, LANES), 0) == lax.broadcasted_iota(
+        jnp.int32, (LANES, LANES), 1
+    )
+    for block in range(rows // LANES):
+        row = slot_ref[block : block + 1, :]
+        slot[pl.ds(block * LANES, LANES)] = jnp.sum(
+            jnp.where(diagonal, row, 0), axis=1, keepdims=True
+        )
     total[...] = jnp.zeros_like(total)
 
     def base(k):
@@ -263,6 +269,19 @@
         def _():
             widen(step, False)
 
+    def sent(first, end):
+        @pl.loop(first, end)
+        def _(step):
+            for part in order:
+                for way in range(2):
+                    ref = piece(owner_slot(step, way, core), part)
+
+                    @pl.when(step + 1 < chips)
+                    def _():
+                        ring(step + 1, way, part, ref).wait_send()
+
+                    pair(step, way, part, ref, core).wait_send()
+
     @pl.loop(0, chunks)
     def _(k):
         tok_load(k).wait()
@@ -277,6 +296,11 @@
         @pl.when(unit == last)
         def _():
             apply(before, before_k)
+            for part in order:
+                for way in range(2):
+                    ring(1, way, part, own_piece(way, part)).wait_send()
+                    pair(0, way, part, own_piece(way, part), core).wait_send()
+            sent(1, chips - 2)
 
         @pl.when(k == 0)
         def _():
@@ -297,22 +321,7 @@
     shrink(chips - 1, chunks - 1)
     widen(chips - 1, True)
 
-    for part in order:
-        for way in range(2):
-            ring(1, way, part, own_piece(way, part)).wait_send()
-            pair(0, way, part, own_piece(way, part), core).wait_send()
-
-    @pl.loop(1, chips)
-    def _(step):
-        for part in order:
-            for way in range(2):
-                ref = piece(owner_slot(step, way, core), part)
-
-                @pl.when(step + 1 < chips)
-                def _():
-                    ring(step + 1, way, part, ref).wait_send()
-
-                pair(step, way, part, ref, core).wait_send()
+    sent(chips - 2, chips)
 
 
 def ring_shards(
@@ -330,6 +339,9 @@
     adapters = adapter_position.shape[0]
     chips = replicas // 2
     parts = CHUNKS + 1
+    ids = jnp.arange(adapters, dtype=jnp.int32)[:, None, None]
+    named = token_adapter.reshape(1, rows // LANES, LANES) == ids
+    slots = jnp.sum(jnp.where(named, adapter_position[:, None, None], 0), axis=0)
     any_space = pl.BlockSpec(memory_space=pl.ANY)
     vmem = pl.BlockSpec(memory_space=pltpu.VMEM)
     dma = pltpu.SemaphoreType.DMA
@@ -340,7 +352,7 @@
             jax.ShapeDtypeStruct((adapters, rank, width), jnp.bfloat16),
             jax.ShapeDtypeStruct((adapters, rank, features), jnp.bfloat16),
         ),
-        in_specs=[any_space] * 4 + [vmem] * 2,
+        in_specs=[any_space] * 4 + [vmem],
         out_specs=(vmem, any_space, any_space),
         scratch_shapes=[
             pltpu.VMEM((rows, width), jnp.bfloat16),
@@ -373,8 +385,7 @@
         value_weight,
         adapter_down_weight,
         adapter_up_weight,
-        token_adapter,
-        adapter_position[None, :],
+        slots,
     )
     alive = jnp.arange(rows, dtype=jnp.int32) < replica_live_rows[0]
     return jnp.where(alive[:, None], values, jnp.zeros_like(values))

time: 199 us -> 198 us (level)
  no operation moved by 1% of the time
where the time goes in v3:
time: 198 us; the launch traced here: 197 us
  Pallas kernels  192 us (97%)
  other arithmetic  3.94 us (2%)
    pallas_call x1, Pallas kernels, ring_shards(): pl.pallas_call(functools.partial(gather_kernel, replicas, rank), out_shap...  192 us

profile of v3, /device:TPU:0, one launch (start us, length us, event | category | flops | bytes accessed | tf_op | source)
XLA Modules:
  0.0 197.5 jit_solution(214745342679808403)
XLA Ops:
  0.0 0.8 select_reduce_fusion.slot_ref
  0.8 0.0 copy-start
  0.8 0.9 copy-done
  1.8 191.9 %gather_and_project.1 = (bf16[1024,1024]{1,0:T(8,128)(2,1)}, bf16[32,64,8192]{2,1,0:T(8,128)(2,1)}, bf16[32,64,1024]{2,1,0:T(8,128)(2,1)}) custom-call(bf16[1024,8192]{1,0:T(8,128)(2,1)} %tok_hbm.1, bf16[8192,1024]{1,0:T(8,128)(2,1)} %weight_hbm.1, bf16[2,64,8192]{2,1,0:T(8,128)(2,1)} %down_hbm.1, bf16[2,64,1024]{2,1,0:T(8,128)(2,1)S(1)} %copy-done, ...), custom_call_target="tpu_custom_call" | custom-call | flops 55834574848 | bytes 134217728 | tf_op jit(solution)/shard_map/gather_and_project/pallas_call | solution.py:348
  194.4 3.1 %broadcast_select_fusion = bf16[1024,1024]{1,0:T(8,128)(2,1)} fusion(bf16[1024,1024]{1,0:T(8,128)(2,1)} %get-tuple-element.6, pred[1024]{0:T(1024)(128)(4,1)S(1)} %iota_compare_fusion.1), kind=kLoop, calls=%fused_computation | loop fusion | flops 1048576 | bytes 4195328 | tf_op jit(solution)/shard_map/jit(_where)/select_n | solution.py:391
  (1 shorter events, 0.0 us)
Async XLA Ops:
  0.8 1.0 copy-start
